TPU v7x, 512 devices: a whole 4x8x8 slice. The times are simulated.
512 devices in a mesh: fsdp: 64 (over y, z), tp: 8 (over x, core).
Axes of the slice: x: 4, y: 8, z: 8, core: 2. Of those that a mesh axis runs over, the one named last changes fastest.
Arguments:
- hidden_prev: bfloat16 [12288, 2048], P('fsdp', 'tp'), may hold values from -6 to 6
- next_ids: int32 [12288], P('fsdp'), may hold values from 0 to 8191
- embed_table: bfloat16 [8192, 2048], P('fsdp', 'tp'), may hold values from -6 to 6
- embed_gain: float32 [2048], P('tp'), may hold values from 0.5 to 1.5
- hidden_gain: float32 [2048], P('tp'), may hold values from 0.5 to 1.5
- join_embed: bfloat16 [2048, 2048], P('tp', 'fsdp'), may hold values from -0.09375 to 0.09375
- join_hidden: bfloat16 [2048, 2048], P('tp', 'fsdp'), may hold values from -0.09375 to 0.09375
- final_gain: float32 [2048], replicated, may hold values from 0.5 to 1.5
- head: bfloat16 [2048, 16384], P('fsdp', 'tp'), may hold values from -7.6 to 7.6
Outputs:
- log_probs: float32 [12288, 16384], P('fsdp', 'tp')
All inputs are finite; a program needn't handle non-finite values.
Results may differ from a plain program's by a relative error of at most 0.0035.
Values may be sent and summed in bfloat16 or wider, within the bound.
No kernel may reach another device: no remote copies, remote signals or barrier semaphores. Data moves between devices by JAX's collectives and lax.ppermute only.
A program may use at most 64 MiB of HBM per device.

v0:
```python
import jax
import jax.numpy as jnp
from jax import lax
from jax.sharding import PartitionSpec as P

D = 2048


eps = 1e-06


def scaled_norm(values, squares, gain):
    return (values.astype(jnp.float32) * lax.rsqrt(squares / D + eps) * gain).astype(jnp.bfloat16)


def final_norm(joined, final_gain):
    wide = joined.astype(jnp.float32)
    mean_sq = jnp.mean(wide * wide, axis=-1, keepdims=True)
    return (wide * lax.rsqrt(mean_sq + eps) * final_gain).astype(jnp.bfloat16)


def shards(
    hidden_prev,
    next_ids,
    embed_table,
    embed_gain,
    hidden_gain,
    join_embed,
    join_hidden,
    final_gain,
    head,
):
    piece = lax.all_gather(embed_table, "fsdp", axis=0, tiled=True)
    positions = lax.iota(jnp.int32, piece.shape[0])
    one_hot = (next_ids[:, None] == positions[None, :]).astype(jnp.bfloat16)
    embedded = jnp.dot(one_hot, piece, preferred_element_type=jnp.float32).astype(jnp.bfloat16)
    embed_wide = embedded.astype(jnp.float32)
    hidden_wide = hidden_prev.astype(jnp.float32)
    embed_sq, hidden_sq = lax.psum(
        (
            jnp.sum(embed_wide * embed_wide, axis=1, keepdims=True),
            jnp.sum(hidden_wide * hidden_wide, axis=1, keepdims=True),
        ),
        "tp",
    )
    embed_norm = scaled_norm(embedded, embed_sq, embed_gain)
    hidden_norm = scaled_norm(hidden_prev, hidden_sq, hidden_gain)
    embed_proj, hidden_proj = (
        lax.all_gather(join_embed, "fsdp", axis=1, tiled=True),
        lax.all_gather(join_hidden, "fsdp", axis=1, tiled=True),
    )
    joined_part = lax.psum_scatter(
        jnp.dot(embed_norm, embed_proj, preferred_element_type=jnp.float32)
        + jnp.dot(hidden_norm, hidden_proj, preferred_element_type=jnp.float32),
        "tp",
        scatter_dimension=0,
        tiled=True,
    ).astype(jnp.bfloat16)
    final = lax.all_gather(final_norm(joined_part, final_gain), "tp", axis=0, tiled=True)
    logits = jnp.dot(
        final, lax.all_gather(head, "fsdp", axis=0, tiled=True), preferred_element_type=jnp.float32
    )
    local_max = jnp.max(logits, axis=1)
    row_highest = lax.pmax(local_max, "tp")
    local_sum = jnp.sum(jnp.exp(logits - row_highest[:, None]), axis=1)
    row_total = lax.psum(local_sum, "tp")
    return logits - row_highest[:, None] - jnp.log(row_total)[:, None]


def solution(mesh):
    return jax.shard_map(
        shards,
        mesh=mesh,
        in_specs=(
            P("fsdp", "tp"),
            P("fsdp"),
            P("fsdp", "tp"),
            P("tp"),
            P("tp"),
            P("tp", "fsdp"),
            P("tp", "fsdp"),
            P(),
            P("fsdp", "tp"),
        ),
        out_specs=P("fsdp", "tp"),
        check_vma=False,
    )
```

profile of v0, /device:TPU:1, one launch (start us, length us, event | category | flops | bytes accessed | tf_op | source)
XLA Modules:
  0.0 446.4 jit_solution(14947951545561460375)
XLA Ops:
  6.5 0.0 all-gather.5.cloned.1.call-start
  6.5 0.7 all-gather.5.cloned.1.call-update
  7.3 0.0 all-gather.7.cloned.1.call-start
  7.3 0.7 all-gather.7.cloned.1.call-update
  8.0 0.0 all-gather.9.cloned.1.call-start
  8.1 0.7 all-gather.9.cloned.1.call-update
  8.7 0.0 reduce-scatter.2.cloned.1.call-start
  8.8 1.0 fusion.4
  9.8 0.0 copy-start.2
  9.8 89.3 %all-gather.5.cloned.1.call-done = bf16[8192,256]{1,0:T(8,128)(2,1)} async-done(((bf16[128,256]{1,0:T(8,128)(2,1)}), bf16[8192,256]{1,0:T(8,128)(2,1)}) %all-gather.5.cloned.1.call-update) | async-done | bytes 4194320 | tf_op jit(solution)/shard_map/all_gather | solution.py:33
  99.1 3.3 multiply_reduce_fusion
  102.5 0.0 copy-start
  102.5 0.0 copy-start.3
  102.5 16.5 %all-reduce = (f32[192,1]{0,1:T(1,128)S(1)}, f32[192,1]{0,1:T(1,128)S(1)}) all-reduce(f32[192,1]{0,1:T(1,128)S(1)} %bitcast.12, f32[192,1]{0,1:T(1,128)S(1)} %bitcast.10), channel_id=1, replica_groups=mesh['fsdp'=64,'tp'=8] {'tp'}, use_global_device_ids=true, to_apply=%region_1.0 | all-reduce | flops 384 | bytes 3072 | tf_op jit(solution)/shard_map/psum | solution.py:39
  119.0 61.3 %all-gather.7.cloned.1.call-done = bf16[256,2048]{0,1:T(8,128)(2,1)} async-done(((bf16[256,32]{0,1:T(8,128)(2,1)}), bf16[256,2048]{0,1:T(8,128)(2,1)}) %all-gather.7.cloned.1.call-update) | async-done | bytes 1048592 | tf_op jit(solution)/shard_map/all_gather | solution.py:49
  180.3 0.0 copy-done.2
  180.3 1.7 fusion.10
  182.0 80.2 %all-gather.9.cloned.1.call-done = bf16[256,2048]{0,1:T(8,128)(2,1)} async-done(((bf16[256,32]{0,1:T(8,128)(2,1)}), bf16[256,2048]{0,1:T(8,128)(2,1)}) %all-gather.9.cloned.1.call-update) | async-done | bytes 1048592 | tf_op jit(solution)/shard_map/all_gather | solution.py:50
  262.2 0.0 copy-done
  262.2 0.0 copy-done.3
  262.2 2.9 convolution_add_fusion
  265.1 0.0 copy-start.1
  265.1 0.0 reduce-scatter.2.cloned.1.call-update
  265.1 0.0 all-gather.11.cloned.1.call-start
  265.2 0.5 all-gather.11.cloned.1.call-update
  265.7 37.2 %reduce-scatter.2.cloned.1.call-done = f32[24,2048]{1,0:T(8,128)} async-done(((f32[192,2048]{1,0:T(8,128)}), f32[24,2048]{1,0:T(8,128)}) %reduce-scatter.2.cloned.1.call-update) | async-done | bytes 196624 | tf_op jit(solution)/shard_map/reduce_scatter | solution.py:52
  302.9 1.1 fusion.7
  304.0 0.0 copy-done.1
  304.0 1.0 fusion.9
  305.0 15.6 %all_gather.18 = bf16[192,2048]{1,0:T(8,128)(2,1)S(1)} all-gather(bf16[24,2048]{1,0:T(8,128)(2,1)S(1)} %fusion.9), channel_id=1, replica_groups=mesh['fsdp'=64,'tp'=8] {'tp'}, dimensions={0}, use_global_device_ids=true | all-gather | bytes 884736 | tf_op jit(solution)/shard_map/all_gather | solution.py:59
  320.6 85.2 %all-gather.11.cloned.1.call-done = bf16[2048,2048]{1,0:T(8,128)(2,1)} async-done(((bf16[32,2048]{1,0:T(8,128)(2,1)}), bf16[2048,2048]{1,0:T(8,128)(2,1)}) %all-gather.11.cloned.1.call-update) | async-done | bytes 8388624 | tf_op jit(solution)/shard_map/all_gather | solution.py:61
  405.8 5.3 %fusion.16 = (f32[192]{0:T(256)S(1)}, f32[192,2048]{1,0:T(8,128)S(1)}) fusion(bf16[192,2048]{1,0:T(8,128)(2,1)S(1)} %all_gather.18, bf16[2048,2048]{1,0:T(8,128)(2,1)} %all-gather.11.cloned.1.call-done), kind=kOutput, calls=%fused_computation.28 | convolution fusion | flops 1611005696 | bytes 10748672 | tf_op jit(solution)/shard_map/dot_general | solution.py:60
  411.1 12.5 %pmax.7 = f32[192]{0:T(256)S(1)} all-reduce(f32[192]{0:T(256)S(1)} %get-tuple-element.9), channel_id=1, replica_groups=mesh['fsdp'=64,'tp'=8] {'tp'}, use_global_device_ids=true, to_apply=%region_7.0 | all-reduce | flops 192 | bytes 1536 | tf_op jit(solution)/shard_map/pmax | solution.py:64
  423.5 0.4 exponential_reduce_fusion
  423.9 14.5 %psum.23 = f32[192]{0:T(256)S(1)} all-reduce(f32[192]{0:T(256)S(1)} %exponential_reduce_fusion), channel_id=1, replica_groups=mesh['fsdp'=64,'tp'=8] {'tp'}, use_global_device_ids=true, to_apply=%region_9.0 | all-reduce | flops 192 | bytes 1536 | tf_op jit(solution)/shard_map/psum | solution.py:66
  438.4 1.4 subtract_subtract_fusion
  (4 shorter events, 0.0 us)
Async XLA Ops:
  6.5 92.6 %all-gather.5.cloned.1.call-start = ((), (), s32[]{:S(2)}) async-start(), calls=%async_computation.1 | async-start | bytes 4259840 | tf_op jit(solution)/shard_map/all_gather | solution.py:33
  7.3 173.1 %all-gather.7.cloned.1.call-start = ((), (), s32[]{:S(2)}) async-start(), calls=%async_computation.2 | async-start | bytes 1064960 | tf_op jit(solution)/shard_map/all_gather | solution.py:49
  8.0 254.2 %all-gather.9.cloned.1.call-start = ((), (), s32[]{:S(2)}) async-start(), calls=%async_computation.3 | async-start | bytes 1064960 | tf_op jit(solution)/shard_map/all_gather | solution.py:50
  8.7 294.2 %reduce-scatter.2.cloned.1.call-start = ((), (), s32[]{:S(2)}) async-start(), calls=%async_computation.4 | async-start | bytes 1769472 | tf_op jit(solution)/shard_map/reduce_scatter | solution.py:52
  9.8 170.5 %copy-start.2 = (f32[256]{0:T(256)S(1)}, f32[256]{0:T(256)}, u32[]{:S(2)}) copy-start(f32[256]{0:T(256)} %param.12) | copy-start | bytes 3076
  102.5 159.8 %copy-start = (bf16[192,256]{1,0:T(8,128)(2,1)S(1)}, bf16[192,256]{1,0:T(8,128)(2,1)}, u32[]{:S(2)}) copy-start(bf16[192,256]{1,0:T(8,128)(2,1)} %param.9) | copy-start | bytes 294916
  102.5 159.8 %copy-start.3 = (f32[256]{0:T(256)S(1)}, f32[256]{0:T(256)}, u32[]{:S(2)}) copy-start(f32[256]{0:T(256)} %param.13) | copy-start | bytes 3076
  265.1 38.8 %copy-start.1 = (f32[2048]{0:T(1024)S(1)}, f32[2048]{0:T(1024)}, u32[]{:S(2)}) copy-start(f32[2048]{0:T(1024)} %param.16) | copy-start | bytes 24580
  265.1 140.7 %all-gather.11.cloned.1.call-start = ((), (), s32[]{:S(2)}) async-start(), calls=%async_computation.5 | async-start | bytes 8519680 | tf_op jit(solution)/shard_map/all_gather | solution.py:61
Sparse Core Ops, SparseCore 0:
  10.4 88.7 all-gather.4
  102.2 78.1 all-gather.6
  183.3 78.8 all-gather.8
  265.3 37.5 reduce-scatter.1
  305.8 99.9 all-gather.10
where the time goes:
time: 447 us; the launch traced here: 446 us
  waiting for transfers between devices  356 us (80%)
  blocking collectives  59.1 us (13%)
  matrix products  13.2 us (3%)
  between operations  13.2 us (3%)
  other arithmetic  4.86 us (1%)
    all_gather x1, waiting for transfers between devices, shards(): piece = lax.all_gather(embed_table, 'fsdp', axis=0, tiled=True)  89.3 us
    all_gather x1, waiting for transfers between devices, shards(): lax.all_gather(head, 'fsdp', axis=0, tiled=True)  85.2 us
    all_gather x1, waiting for transfers between devices, shards(): lax.all_gather(join_hidden, 'fsdp', axis=1, tiled=True)  80.2 us
    all_gather x1, waiting for transfers between devices, shards(): lax.all_gather(join_embed, 'fsdp', axis=1, tiled=True)  61.3 us
    reduce_scatter x1, waiting for transfers between devices, shards(): lax.psum_scatter(jnp.dot(embed_norm, embed_proj, preferred_element_type=j...  37.2 us
    psum x1, blocking collectives, shards(): lax.psum((jnp.sum(embed_wide * embed_wide, axis=1, keepdims=True), jnp.su...  16.5 us
    all_gather x1, blocking collectives, shards(): lax.all_gather(final_norm(joined_part, final_gain), 'tp', axis=0, tiled=T...  15.6 us
    psum x1, blocking collectives, shards(): row_total = lax.psum(local_sum, 'tp')  14.5 us
  transfers between devices with their start and end apart: 5, of which 5 were waited for; matrix products, arithmetic and copies ran while one was open for 2% of the time, Pallas kernels for 0%

commit v1 on v0

v1 whole, which is shorter than its diff:
```python
import jax
import jax.numpy as jnp
from jax import lax
from jax.experimental import pallas as pl
from jax.experimental.pallas import tpu as pltpu
from jax.sharding import Mesh, PartitionSpec as P

D = 2048
eps = 1e-06
FS = ("y", "z")
TP = ("x", "core")
NY, NZ, NT = 8, 8, 8
f32 = jnp.float32
bf16 = jnp.bfloat16
CONTRACT = (((1,), (1,)), ((), ()))
UP = [(i, (i + 1) % NY) for i in range(NY)]
DOWN = [(i, (i - 1) % NY) for i in range(NY)]


def scaled(values, squares, gain):
    return (values.astype(f32) * lax.rsqrt(squares / D + eps) * gain).astype(bf16)


def row_squares(values):
    wide = values.astype(f32)
    return jnp.sum(wide * wide, axis=1)


def spread(block, axes, count):
    copies = jnp.broadcast_to(block[None], (count,) + block.shape)
    return lax.all_to_all(copies, axes, 0, 0, tiled=True)


def join_kernel(found_ref, hidden_ref, *refs):
    out_ref = refs[-1]
    embed = found_ref[0].astype(f32)
    for k in range(1, found_ref.shape[0]):
        embed = embed + found_ref[k].astype(f32)
    embed = embed.astype(bf16)
    hidden = hidden_ref[...]
    width = hidden.shape[1]
    for j, ref in enumerate(refs[:-1]):
        cols = ref.shape[1] // 2
        count = ref.shape[0] * cols
        embed_proj = ref[:, :cols, :].reshape(count, width)
        hidden_proj = ref[:, cols:, :].reshape(count, width)
        total = lax.dot_general(embed, embed_proj, CONTRACT, preferred_element_type=f32)
        total += lax.dot_general(hidden, hidden_proj, CONTRACT, preferred_element_type=f32)
        out_ref[:, j * count : (j + 1) * count] = total.astype(bf16)


def join(found, hidden, blocks):
    rows = hidden.shape[0]
    return pl.pallas_call(
        join_kernel,
        out_shape=jax.ShapeDtypeStruct((rows, D), bf16),
        in_specs=[pl.BlockSpec(memory_space=pltpu.VMEM)] * (2 + len(blocks)),
        out_specs=pl.BlockSpec(memory_space=pltpu.VMEM),
        compiler_params=pltpu.CompilerParams(vmem_limit_bytes=16 * 2**20),
        cost_estimate=pl.CostEstimate(flops=4 * rows * 256 * D, bytes_accessed=4 * 2**20, transcendentals=0),
    )(found, hidden, *blocks)


def shards(hidden_prev, next_ids, embed_table, embed_gain, hidden_gain, join_embed, join_hidden, final_gain, head):
    rows = next_ids.shape[0]
    width = hidden_prev.shape[1]
    vocab = embed_table.shape[0]

    head_all = lax.all_gather(head, FS, axis=0, tiled=True)

    low = jnp.stack([next_ids // 64, next_ids % 64]).astype(bf16)
    low = jnp.pad(low, ((0, 14), (0, width - rows)))
    line = spread(jnp.concatenate([join_embed.T, join_hidden.T, low], axis=0), "z", NZ)
    part = lax.all_gather(embed_table, "y", axis=0, tiled=True)
    line, part = lax.optimization_barrier((line, part))
    cols = 2 * join_embed.shape[1]
    low = line[:, cols : cols + 2, :rows].astype(jnp.int32)
    ids = (low[:, 0] * 64 + low[:, 1]).reshape(-1)
    line = line[:, :cols]

    down, up = lax.ppermute(line, "y", DOWN), lax.ppermute(line, "y", UP)
    squares = lax.psum(jnp.concatenate([row_squares(part), row_squares(hidden_prev)]), TP)
    down, up, squares = lax.optimization_barrier((down, up, squares))
    down2, up2 = lax.ppermute(down, "y", DOWN), lax.ppermute(up, "y", UP)
    table_norm = scaled(part, squares[: NY * vocab, None], embed_gain)
    hidden_norm = scaled(hidden_prev, squares[NY * vocab :, None], hidden_gain)
    row = lax.iota(jnp.int32, NY * vocab)
    place = (row // vocab * NZ + lax.axis_index("z")) * vocab + row % vocab
    one_hot = (ids[:, None] == place[None, :]).astype(bf16)
    found = jnp.dot(one_hot, table_norm, preferred_element_type=f32).astype(bf16)
    found = lax.all_to_all(found.reshape(NZ, rows, width), "z", 0, 0, tiled=True)
    down3, up3 = lax.ppermute(down2, "y", DOWN), lax.ppermute(up2, "y", UP)
    up4 = lax.ppermute(up3, "y", UP)
    blocks = [line, down, down2, down3, up4, up3, up2, up]

    share = join(found, hidden_norm, blocks)
    shares = lax.all_to_all(share.reshape(NT, rows // NT, D), TP, 0, 0, tiled=True)
    joined = jnp.sum(shares.astype(f32), axis=0).astype(bf16)
    twice = jnp.concatenate([joined, joined], axis=1)
    joined = lax.dynamic_slice_in_dim(twice, (NY - lax.axis_index("y")) % NY * (D // NY), D, axis=1)
    final_part = scaled(joined, row_squares(joined)[:, None], final_gain)
    final = lax.all_gather(final_part, TP, axis=0, tiled=True)

    logits = jnp.dot(final, head_all, preferred_element_type=f32)
    local_max = jnp.max(logits, axis=1)
    local_sum = jnp.sum(jnp.exp(logits - local_max[:, None]), axis=1)
    both = spread(jnp.stack([local_max, local_sum]), TP, NT)
    highest = jnp.max(both[:, 0], axis=0)
    total = jnp.sum(both[:, 1] * jnp.exp(both[:, 0] - highest), axis=0)
    return logits - highest[:, None] - jnp.log(total)[:, None]


def solution(mesh):
    mesh = Mesh(mesh.devices.reshape(NY, NZ, NT // 2, 2), FS + TP)
    return jax.shard_map(
        shards,
        mesh=mesh,
        in_specs=(
            P(FS, TP),
            P(FS),
            P(FS, TP),
            P(TP),
            P(TP),
            P(TP, FS),
            P(TP, FS),
            P(),
            P(FS, TP),
        ),
        out_specs=P(FS, TP),
        check_vma=False,
    )
```

time: 447 us -> 181 us (0.40)
  waiting for transfers between devices: 356 us -> 40.3 us
  starting transfers between devices: 0.16 us -> 48 us
  matrix products: 13.2 us -> 7.41 us
    all_gather x4 -> x1, waiting for transfers between devices: 316 us -> 0.01 us  [shards(): head_all = lax.all_gather(head, FS, axis=0, tiled=True)]
    reduce_scatter x1 -> x0, waiting for transfers between devices: 37.2 us -> none  [shards(): lax.psum_scatter(jnp.dot(embed_norm, embed_proj, preferred_element_type=j...]
    all_to_all x0 -> x3, starting transfers between devices: none -> 27.8 us  [the longest x1 10.9 us: spread(): return lax.all_to_all(copies, axes, 0, 0, tiled=True)]
    ppermute x0 -> x7, waiting for transfers between devices: none -> 27.3 us  [the longest x1 10.4 us: shards(): up4 = lax.ppermute(up3, 'y', UP)]
    all_gather x1 -> x2, blocking collectives: 15.6 us -> 37.5 us  [the longest x1 23.3 us: shards(): part = lax.all_gather(embed_table, 'y', axis=0, tiled=True)]
    ppermute x0 -> x7, starting transfers between devices: none -> 20.2 us  [the longest x2 6.48 us: shards(): down3, up3 = (lax.ppermute(down2, 'y', DOWN), lax.ppermute(up2, 'y', UP))]
    psum x2 -> x1, blocking collectives: 31 us -> 18.1 us  [shards(): lax.psum(jnp.concatenate([row_squares(part), row_squares(hidden_prev)]), TP)]
    pmax x1 -> x0, blocking collectives: 12.5 us -> none  [shards(): row_highest = lax.pmax(local_max, 'tp')]
  transfers between devices with their start and end apart: 5 -> 11, of which waited for: 5 -> 5; matrix products, arithmetic and copies ran while one was open for 2% -> 3% of each run, Pallas kernels for 0% -> 1%
where the time goes in v1:
time: 181 us; the launch traced here: 180 us
  blocking collectives  62.9 us (35%)
  starting transfers between devices  48 us (27%)
  waiting for transfers between devices  40.3 us (22%)
  between operations  13.6 us (8%)
  matrix products  7.41 us (4%)
  other arithmetic  5.15 us (3%)
    all_gather x1, blocking collectives, shards(): part = lax.all_gather(embed_table, 'y', axis=0, tiled=True)  23.3 us
    psum x1, blocking collectives, shards(): lax.psum(jnp.concatenate([row_squares(part), row_squares(hidden_prev)]), TP)  18.1 us
    all_gather x1, blocking collectives, shards(): final = lax.all_gather(final_part, TP, axis=0, tiled=True)  14.2 us
    all_to_all x1, waiting for transfers between devices, shards(): lax.all_to_all(share.reshape(NT, rows // NT, D), TP, 0, 0, tiled=True)  12.3 us
    all_to_all x1, starting transfers between devices, spread(): return lax.all_to_all(copies, axes, 0, 0, tiled=True)  10.9 us
    ppermute x1, waiting for transfers between devices, shards(): up4 = lax.ppermute(up3, 'y', UP)  10.4 us
    ppermute x2, waiting for transfers between devices, shards(): down2, up2 = (lax.ppermute(down, 'y', DOWN), lax.ppermute(up, 'y', UP))  9.79 us
    all_to_all x1, starting transfers between devices, shards(): lax.all_to_all(share.reshape(NT, rows // NT, D), TP, 0, 0, tiled=True)  9.71 us
  transfers between devices with their start and end apart: 11, of which 5 were waited for; matrix products, arithmetic and copies ran while one was open for 3% of the time, Pallas kernels for 1%

profile of v1, /device:TPU:1, one launch (start us, length us, event | category | flops | bytes accessed | tf_op | source)
XLA Modules:
  0.0 180.0 jit_solution(18427730577755177193)
XLA Ops:
  6.5 0.0 copy-start.3
  6.5 0.0 all-gather.2.cloned.1.call-start
  6.5 0.7 all-gather.2.cloned.1.call-update
  7.3 0.7 fusion.43
  8.0 0.7 pad_maximum_fusion
  8.7 0.7 broadcast_in_dim.4
  9.5 10.9 %all-to-all-start = ((bf16[8,80,256]{2,1,0:T(8,128)(2,1)}), bf16[8,80,256]{2,1,0:T(8,128)(2,1)S(1)}, u32[]{:S(2)}, u32[]{:S(2)}) async-start(bf16[8,80,256]{2,1,0:T(8,128)(2,1)} %broadcast_in_dim.4), calls=%async_computation | async-start | bytes 655360 | tf_op jit(solution)/shard_map/all_to_all | solution.py:31
  20.3 1.0 fusion.13
  21.4 23.3 %all_gather.9 = bf16[1024,256]{1,0:T(8,128)(2,1)S(1)} all-gather(bf16[128,256]{1,0:T(8,128)(2,1)} %param.11), channel_id=1, replica_groups=mesh['y'=8,'z'=8,'x'=4,'core'=2] {'y'}, dimensions={0}, use_global_device_ids=true | all-gather | bytes 589824 | tf_op jit(solution)/shard_map/all_gather | solution.py:74
  44.6 0.0 all-to-all-done
  44.7 3.3 %collective-permute-start = (bf16[8,64,256]{2,1,0:T(8,128)(2,1)S(1)}, bf16[8,64,256]{2,1,0:T(8,128)(2,1)S(1)}, u32[]{:S(2)}, u32[]{:S(2)}) collective-permute-start(bf16[8,64,256]{2,1,0:T(8,128)(2,1)S(1)} %slice.28.refs_0_), channel_id=1, source_target_pairs={{0,448},{64,0},{128,64},{192,128},{256,192},{320,256},{384,320},{4... | collective-permute-start | bytes 786440 | tf_op jit(solution)/shard_map/ppermute | solution.py:81
  48.0 1.9 %collective-permute-start.1 = (bf16[8,64,256]{2,1,0:T(8,128)(2,1)S(1)}, bf16[8,64,256]{2,1,0:T(8,128)(2,1)S(1)}, u32[]{:S(2)}, u32[]{:S(2)}) collective-permute-start(bf16[8,64,256]{2,1,0:T(8,128)(2,1)S(1)} %slice.28.refs_0_), channel_id=1, source_target_pairs={{0,64},{64,128},{128,192},{192,256},{256,320},{320,384},{384,448},... | collective-permute-start | bytes 786440 | tf_op jit(solution)/shard_map/ppermute | solution.py:81
  50.0 0.1 add.84
  50.1 0.2 fusion.7
  50.3 18.1 %psum.7 = f32[1216]{0:T(1024)S(1)} all-reduce(f32[1216]{0:T(1024)S(1)} %pad_maximum_fusion.1), channel_id=1, replica_groups=mesh['y'=8,'z'=8,'x'=4,'core'=2] {'x','core'}, use_global_device_ids=true, to_apply=%region_2.3 | all-reduce | flops 1216 | bytes 9728 | tf_op jit(solution)/shard_map/psum | solution.py:82
  68.4 0.0 collective-permute-done.refs_1_
  68.4 0.0 collective-permute-done.1.refs_7_
  68.4 0.0 copy-done.3
  68.4 2.1 %fusion.4 = bf16[1536,256]{1,0:T(8,128)(2,1)} fusion(s32[1024]{0:T(1024)S(1)} %fusion.40, s32[1536]{0:T(1024)S(1)} %add.84, bf16[1024,256]{1,0:T(8,128)(2,1)S(1)} %all_gather.9, f32[256]{0:T(256)S(1)} %copy-done.3, f32[1024]{0:T(1024)S(1)} %add_rsqrt_fusion), kind=kOutput, calls=%fused_computation.4 | convolution fusion | flops 808321024 | bytes 1326080 | tf_op jit(solution)/shard_map/dot_general | solution.py:90
  70.6 0.0 copy-start
  70.6 0.0 copy-start.2
  70.6 7.3 %all-to-all-start.1 = ((bf16[8,192,256]{2,1,0:T(8,128)(2,1)}), bf16[8,192,256]{2,1,0:T(8,128)(2,1)S(1)}, u32[]{:S(2)}, u32[]{:S(2)}) async-start(bf16[8,192,256]{2,1,0:T(8,128)(2,1)} %bitcast.2), calls=%async_computation.1 | async-start | bytes 1572864 | tf_op jit(solution)/shard_map/all_to_all | solution.py:91
  77.8 2.3 %collective-permute-start.4 = (bf16[8,64,256]{2,1,0:T(8,128)(2,1)S(1)}, bf16[8,64,256]{2,1,0:T(8,128)(2,1)S(1)}, u32[]{:S(2)}, u32[]{:S(2)}) collective-permute-start(bf16[8,64,256]{2,1,0:T(8,128)(2,1)S(1)} %collective-permute-done.1.refs_7_), channel_id=1, source_target_pairs={{0,64},{64,128},{128,192},{192,256},{256,320},{320,384},{384,448},... | collective-permute-start | bytes 786440 | tf_op jit(solution)/shard_map/ppermute | solution.py:84
  80.2 4.2 %collective-permute-start.2 = (bf16[8,64,256]{2,1,0:T(8,128)(2,1)S(1)}, bf16[8,64,256]{2,1,0:T(8,128)(2,1)S(1)}, u32[]{:S(2)}, u32[]{:S(2)}) collective-permute-start(bf16[8,64,256]{2,1,0:T(8,128)(2,1)S(1)} %collective-permute-done.refs_1_), channel_id=1, source_target_pairs={{0,448},{64,0},{128,64},{192,128},{256,192},{320,256},{384,320},{4... | collective-permute-start | bytes 786440 | tf_op jit(solution)/shard_map/ppermute | solution.py:84
  84.3 9.8 %collective-permute-done.4.refs_6_ = bf16[8,64,256]{2,1,0:T(8,128)(2,1)S(1)} collective-permute-done((bf16[8,64,256]{2,1,0:T(8,128)(2,1)S(1)}, bf16[8,64,256]{2,1,0:T(8,128)(2,1)S(1)}, u32[]{:S(2)}, u32[]{:S(2)}) %collective-permute-start.4) | collective-permute-done | bytes 262176 | tf_op jit(solution)/shard_map/ppermute | solution.py:84
  94.1 1.9 %collective-permute-start.5 = (bf16[8,64,256]{2,1,0:T(8,128)(2,1)S(1)}, bf16[8,64,256]{2,1,0:T(8,128)(2,1)S(1)}, u32[]{:S(2)}, u32[]{:S(2)}) collective-permute-start(bf16[8,64,256]{2,1,0:T(8,128)(2,1)S(1)} %collective-permute-done.4.refs_6_), channel_id=1, source_target_pairs={{0,64},{64,128},{128,192},{192,256},{256,320},{320,384},{384,448},... | collective-permute-start | bytes 786440 | tf_op jit(solution)/shard_map/ppermute | solution.py:92
  96.0 0.0 collective-permute-done.2.refs_2_
  96.1 4.6 %collective-permute-start.3 = (bf16[8,64,256]{2,1,0:T(8,128)(2,1)S(1)}, bf16[8,64,256]{2,1,0:T(8,128)(2,1)S(1)}, u32[]{:S(2)}, u32[]{:S(2)}) collective-permute-start(bf16[8,64,256]{2,1,0:T(8,128)(2,1)S(1)} %collective-permute-done.2.refs_2_), channel_id=1, source_target_pairs={{0,448},{64,0},{128,64},{192,128},{256,192},{320,256},{384,320},{4... | collective-permute-start | bytes 786440 | tf_op jit(solution)/shard_map/ppermute | solution.py:92
  100.6 5.9 %collective-permute-done.5.refs_5_ = bf16[8,64,256]{2,1,0:T(8,128)(2,1)S(1)} collective-permute-done((bf16[8,64,256]{2,1,0:T(8,128)(2,1)S(1)}, bf16[8,64,256]{2,1,0:T(8,128)(2,1)S(1)}, u32[]{:S(2)}, u32[]{:S(2)}) %collective-permute-start.5) | collective-permute-done | bytes 262176 | tf_op jit(solution)/shard_map/ppermute | solution.py:92
  106.5 1.9 %collective-permute-start.6 = (bf16[8,64,256]{2,1,0:T(8,128)(2,1)S(1)}, bf16[8,64,256]{2,1,0:T(8,128)(2,1)S(1)}, u32[]{:S(2)}, u32[]{:S(2)}) collective-permute-start(bf16[8,64,256]{2,1,0:T(8,128)(2,1)S(1)} %collective-permute-done.5.refs_5_), channel_id=1, source_target_pairs={{0,64},{64,128},{128,192},{192,256},{256,320},{320,384},{384,448},... | collective-permute-start | bytes 786440 | tf_op jit(solution)/shard_map/ppermute | solution.py:93
  108.4 0.0 copy-done
  108.4 0.0 copy-done.2
  108.4 0.1 fusion.15.hidden_ref
  108.5 1.2 collective-permute-done.3.refs_3_
  109.8 10.4 %collective-permute-done.6.refs_4_ = bf16[8,64,256]{2,1,0:T(8,128)(2,1)S(1)} collective-permute-done((bf16[8,64,256]{2,1,0:T(8,128)(2,1)S(1)}, bf16[8,64,256]{2,1,0:T(8,128)(2,1)S(1)}, u32[]{:S(2)}, u32[]{:S(2)}) %collective-permute-start.6) | collective-permute-done | bytes 262176 | tf_op jit(solution)/shard_map/ppermute | solution.py:93
  120.2 0.0 all-to-all-done.1.found_ref
  120.2 1.7 shard_map.91
  121.9 0.0 copy-start.1
  121.9 9.7 %all-to-all-start.2 = ((bf16[8,24,2048]{2,1,0:T(8,128)(2,1)}), bf16[8,24,2048]{2,1,0:T(8,128)(2,1)S(1)}, u32[]{:S(2)}, u32[]{:S(2)}) async-start(bf16[8,24,2048]{2,1,0:T(8,128)(2,1)} %bitcast.3), calls=%async_computation.2 | async-start | bytes 1572864 | tf_op jit(solution)/shard_map/all_to_all | solution.py:97
  131.6 12.3 %all-to-all-done.2 = bf16[8,24,2048]{2,1,0:T(8,128)(2,1)S(1)} async-done(((bf16[8,24,2048]{2,1,0:T(8,128)(2,1)}), bf16[8,24,2048]{2,1,0:T(8,128)(2,1)S(1)}, u32[]{:S(2)}, u32[]{:S(2)}) %all-to-all-start.2) | async-done | bytes 786464 | tf_op jit(solution)/shard_map/all_to_all | solution.py:97
  144.0 0.1 reduce_sum.59
  144.1 0.2 fusion.16
  144.3 0.0 copy-done.1
  144.3 0.1 fusion.18
  144.5 14.2 %all_gather.10 = bf16[192,2048]{1,0:T(8,128)(2,1)S(1)} all-gather(bf16[24,2048]{1,0:T(8,128)(2,1)S(1)} %fusion.18), channel_id=1, replica_groups=mesh['y'=8,'z'=8,'x'=4,'core'=2] {'x','core'}, dimensions={0}, use_global_device_ids=true | all-gather | bytes 884736 | tf_op jit(solution)/shard_map/all_gather | solution.py:102
  158.6 0.0 all-gather.2.cloned.1.call-done
  158.7 5.3 %fusion.44 = (f32[192]{0:T(256)S(1)}, f32[192,2048]{1,0:T(8,128)S(1)}) fusion(bf16[192,2048]{1,0:T(8,128)(2,1)S(1)} %all_gather.10, bf16[2048,2048]{1,0:T(8,128)(2,1)} %all-gather.2.cloned.1.call-done), kind=kOutput, calls=%fused_computation.75 | convolution fusion | flops 1611005696 | bytes 10748672 | tf_op jit(solution)/shard_map/dot_general | solution.py:104
  163.9 0.4 exponential_reduce_fusion
  164.3 7.3 %all_to_all.20 = f32[8,2,192]{2,1,0:T(2,128)S(1)} all-to-all(f32[8,2,192]{2,1,0:T(2,128)S(1)} %broadcast_in_dim.5), channel_id=1, replica_groups=mesh['y'=8,'z'=8,'x'=4,'core'=2] {'x','core'}, dimensions={0} | all-to-all | bytes 24576 | tf_op jit(solution)/shard_map/all_to_all | solution.py:31
  171.7 1.4 subtract_subtract_fusion
  (16 shorter events, 0.2 us)
Async XLA Ops:
  6.5 61.9 %copy-start.3 = (f32[256]{0:T(256)S(1)}, f32[256]{0:T(256)}, u32[]{:S(2)}) copy-start(f32[256]{0:T(256)} %param.12) | copy-start | bytes 3076
  6.5 152.1 %all-gather.2.cloned.1.call-start = ((), (), s32[]{:S(2)}) async-start(), calls=%async_computation.4 | async-start | bytes 8519680 | tf_op jit(solution)/shard_map/all_gather | solution.py:69
  9.5 35.2 %all-to-all-start = ((bf16[8,80,256]{2,1,0:T(8,128)(2,1)}), bf16[8,80,256]{2,1,0:T(8,128)(2,1)S(1)}, u32[]{:S(2)}, u32[]{:S(2)}) async-start(bf16[8,80,256]{2,1,0:T(8,128)(2,1)} %broadcast_in_dim.4), calls=%async_computation | async-start | bytes 655360 | tf_op jit(solution)/shard_map/all_to_all | solution.py:31
  44.7 23.7 %collective-permute-start = (bf16[8,64,256]{2,1,0:T(8,128)(2,1)S(1)}, bf16[8,64,256]{2,1,0:T(8,128)(2,1)S(1)}, u32[]{:S(2)}, u32[]{:S(2)}) collective-permute-start(bf16[8,64,256]{2,1,0:T(8,128)(2,1)S(1)} %slice.28.refs_0_), channel_id=1, source_target_pairs={{0,448},{64,0},{128,64},{192,128},{256,192},{320,256},{384,320},{4... | collective-permute-start | bytes 786440 | tf_op jit(solution)/shard_map/ppermute | solution.py:81
  48.0 20.4 %collective-permute-start.1 = (bf16[8,64,256]{2,1,0:T(8,128)(2,1)S(1)}, bf16[8,64,256]{2,1,0:T(8,128)(2,1)S(1)}, u32[]{:S(2)}, u32[]{:S(2)}) collective-permute-start(bf16[8,64,256]{2,1,0:T(8,128)(2,1)S(1)} %slice.28.refs_0_), channel_id=1, source_target_pairs={{0,64},{64,128},{128,192},{192,256},{256,320},{320,384},{384,448},... | collective-permute-start | bytes 786440 | tf_op jit(solution)/shard_map/ppermute | solution.py:81
  70.6 37.8 %copy-start = (bf16[192,256]{1,0:T(8,128)(2,1)S(1)}, bf16[192,256]{1,0:T(8,128)(2,1)}, u32[]{:S(2)}) copy-start(bf16[192,256]{1,0:T(8,128)(2,1)} %param.9) | copy-start | bytes 294916
  70.6 37.9 %copy-start.2 = (f32[256]{0:T(256)S(1)}, f32[256]{0:T(256)}, u32[]{:S(2)}) copy-start(f32[256]{0:T(256)} %param.13) | copy-start | bytes 3076
  70.6 49.6 %all-to-all-start.1 = ((bf16[8,192,256]{2,1,0:T(8,128)(2,1)}), bf16[8,192,256]{2,1,0:T(8,128)(2,1)S(1)}, u32[]{:S(2)}, u32[]{:S(2)}) async-start(bf16[8,192,256]{2,1,0:T(8,128)(2,1)} %bitcast.2), calls=%async_computation.1 | async-start | bytes 1572864 | tf_op jit(solution)/shard_map/all_to_all | solution.py:91
  77.8 16.3 %collective-permute-start.4 = (bf16[8,64,256]{2,1,0:T(8,128)(2,1)S(1)}, bf16[8,64,256]{2,1,0:T(8,128)(2,1)S(1)}, u32[]{:S(2)}, u32[]{:S(2)}) collective-permute-start(bf16[8,64,256]{2,1,0:T(8,128)(2,1)S(1)} %collective-permute-done.1.refs_7_), channel_id=1, source_target_pairs={{0,64},{64,128},{128,192},{192,256},{256,320},{320,384},{384,448},... | collective-permute-start | bytes 786440 | tf_op jit(solution)/shard_map/ppermute | solution.py:84
  80.2 15.9 %collective-permute-start.2 = (bf16[8,64,256]{2,1,0:T(8,128)(2,1)S(1)}, bf16[8,64,256]{2,1,0:T(8,128)(2,1)S(1)}, u32[]{:S(2)}, u32[]{:S(2)}) collective-permute-start(bf16[8,64,256]{2,1,0:T(8,128)(2,1)S(1)} %collective-permute-done.refs_1_), channel_id=1, source_target_pairs={{0,448},{64,0},{128,64},{192,128},{256,192},{320,256},{384,320},{4... | collective-permute-start | bytes 786440 | tf_op jit(solution)/shard_map/ppermute | solution.py:84
  94.1 12.4 %collective-permute-start.5 = (bf16[8,64,256]{2,1,0:T(8,128)(2,1)S(1)}, bf16[8,64,256]{2,1,0:T(8,128)(2,1)S(1)}, u32[]{:S(2)}, u32[]{:S(2)}) collective-permute-start(bf16[8,64,256]{2,1,0:T(8,128)(2,1)S(1)} %collective-permute-done.4.refs_6_), channel_id=1, source_target_pairs={{0,64},{64,128},{128,192},{192,256},{256,320},{320,384},{384,448},... | collective-permute-start | bytes 786440 | tf_op jit(solution)/shard_map/ppermute | solution.py:92
  96.1 13.7 %collective-permute-start.3 = (bf16[8,64,256]{2,1,0:T(8,128)(2,1)S(1)}, bf16[8,64,256]{2,1,0:T(8,128)(2,1)S(1)}, u32[]{:S(2)}, u32[]{:S(2)}) collective-permute-start(bf16[8,64,256]{2,1,0:T(8,128)(2,1)S(1)} %collective-permute-done.2.refs_2_), channel_id=1, source_target_pairs={{0,448},{64,0},{128,64},{192,128},{256,192},{320,256},{384,320},{4... | collective-permute-start | bytes 786440 | tf_op jit(solution)/shard_map/ppermute | solution.py:92
  106.5 13.7 %collective-permute-start.6 = (bf16[8,64,256]{2,1,0:T(8,128)(2,1)S(1)}, bf16[8,64,256]{2,1,0:T(8,128)(2,1)S(1)}, u32[]{:S(2)}, u32[]{:S(2)}) collective-permute-start(bf16[8,64,256]{2,1,0:T(8,128)(2,1)S(1)} %collective-permute-done.5.refs_5_), channel_id=1, source_target_pairs={{0,64},{64,128},{128,192},{192,256},{256,320},{320,384},{384,448},... | collective-permute-start | bytes 786440 | tf_op jit(solution)/shard_map/ppermute | solution.py:93
  121.9 22.4 %copy-start.1 = (f32[2048]{0:T(1024)S(1)}, f32[2048]{0:T(1024)}, u32[]{:S(2)}) copy-start(f32[2048]{0:T(1024)} %param.16) | copy-start | bytes 24580
  121.9 22.0 %all-to-all-start.2 = ((bf16[8,24,2048]{2,1,0:T(8,128)(2,1)}), bf16[8,24,2048]{2,1,0:T(8,128)(2,1)S(1)}, u32[]{:S(2)}, u32[]{:S(2)}) async-start(bf16[8,24,2048]{2,1,0:T(8,128)(2,1)} %bitcast.3), calls=%async_computation.2 | async-start | bytes 1572864 | tf_op jit(solution)/shard_map/all_to_all | solution.py:97
Sparse Core Ops, SparseCore 0:
  10.4 126.0 all-gather.1

commit v2 on v1

v2 whole, which is shorter than its diff:
```python
import jax
import jax.numpy as jnp
from jax import lax
from jax.experimental import pallas as pl
from jax.experimental.pallas import tpu as pltpu
from jax.sharding import Mesh, PartitionSpec as P

D = 2048
eps = 1e-06
FS = ("y", "z")
TP = ("x", "core")
NY, NZ, NT = 8, 8, 8
f32 = jnp.float32
bf16 = jnp.bfloat16
CONTRACT = (((1,), (1,)), ((), ()))
UP = [(i, (i + 1) % NY) for i in range(NY)]
ACROSS = [(i, (i + NY // 2) % NY) for i in range(NY)]
DOWN = [(i, (i - 1) % NY) for i in range(NY)]


def row_squares(values):
    wide = values.astype(f32)
    return jnp.sum(wide * wide, axis=1)


def spread(block, axes, count):
    copies = jnp.broadcast_to(block[None], (count,) + block.shape)
    return lax.all_to_all(copies, axes, 0, 0, tiled=True)


def join_kernel(embed_ref, hidden_ref, embed_scale_ref, hidden_scale_ref, *refs):
    out_ref = refs[-1]
    embed, hidden = embed_ref[...], hidden_ref[...]
    embed_scale, hidden_scale = embed_scale_ref[...], hidden_scale_ref[...]
    width = hidden.shape[1]
    for j, ref in enumerate(refs[:-1]):
        cols = ref.shape[1] // 2
        count = ref.shape[0] * cols
        embed_proj = ref[:, :cols, :].reshape(count, width)
        hidden_proj = ref[:, cols:, :].reshape(count, width)
        total = embed_scale * lax.dot_general(embed, embed_proj, CONTRACT, preferred_element_type=f32)
        total += hidden_scale * lax.dot_general(hidden, hidden_proj, CONTRACT, preferred_element_type=f32)
        out_ref[:, j * count : (j + 1) * count] = total.astype(bf16)


def join(embed, hidden, embed_scale, hidden_scale, blocks):
    rows = hidden.shape[0]
    return pl.pallas_call(
        join_kernel,
        out_shape=jax.ShapeDtypeStruct((rows, D), bf16),
        in_specs=[pl.BlockSpec(memory_space=pltpu.VMEM)] * (4 + len(blocks)),
        out_specs=pl.BlockSpec(memory_space=pltpu.VMEM),
        compiler_params=pltpu.CompilerParams(vmem_limit_bytes=16 * 2**20),
        cost_estimate=pl.CostEstimate(flops=4 * rows * 256 * D, bytes_accessed=4 * 2**20, transcendentals=0),
    )(embed, hidden, embed_scale, hidden_scale, *blocks)


def shards(hidden_prev, next_ids, embed_table, embed_gain, hidden_gain, join_embed, join_hidden, final_gain, head):
    rows = next_ids.shape[0]
    width = hidden_prev.shape[1]
    vocab = embed_table.shape[0]
    cols = 2 * join_embed.shape[1]

    head_all = lax.all_gather(head, FS, axis=0, tiled=True)

    next_ids = next_ids.reshape(NT // 2, 2, rows // NT).swapaxes(0, 1).reshape(rows)
    hidden_prev = hidden_prev.reshape(NT // 2, 2, rows // NT, width).swapaxes(0, 1).reshape(rows, width)

    part = spread(embed_table, "y", NY).reshape(NY * vocab, width)
    low = jnp.stack([next_ids // 64, next_ids % 64]).astype(bf16)
    low = jnp.pad(low, ((0, 14), (0, width - rows)))
    own = jnp.concatenate([join_embed.T, join_hidden.T], axis=0)
    far = lax.ppermute(own, "y", ACROSS)
    line = lax.all_gather(jnp.concatenate([own, far, low], axis=0), "z", axis=0)
    line, part = lax.optimization_barrier((line, part))
    low = line[:, 2 * cols : 2 * cols + 2, :rows].astype(jnp.int32)
    ids = (low[:, 0] * 64 + low[:, 1]).reshape(-1)
    far, line = line[:, cols : 2 * cols], line[:, :cols]

    down, up = lax.ppermute(line, "y", DOWN), lax.ppermute(line, "y", UP)
    row = lax.iota(jnp.int32, NY * vocab)
    place = (row // vocab * NZ + lax.axis_index("z")) * vocab + row % vocab
    one_hot = (ids[:, None] == place[None, :]).astype(bf16)
    found = jnp.dot(one_hot, part, preferred_element_type=f32).astype(bf16)
    found = lax.all_to_all(found.reshape(NZ, rows, width), "z", 0, 0, tiled=True)
    down2, up2 = lax.ppermute(down, "y", DOWN), lax.ppermute(up, "y", UP)
    down3, up3 = lax.ppermute(far, "y", DOWN), lax.ppermute(far, "y", UP)
    blocks = [line, down, down2, up3, far, down3, up2, up]

    embedded = jnp.sum(found.astype(f32), axis=0)
    squares = jnp.stack([row_squares(embedded), row_squares(hidden_prev)])
    squares = lax.psum(squares, TP)
    scales = lax.rsqrt(squares / D + eps)[:, :, None]
    embedded = (embedded * embed_gain).astype(bf16)
    hidden = (hidden_prev.astype(f32) * hidden_gain).astype(bf16)
    share = join(embedded, hidden, scales[0], scales[1], blocks)
    pair = lax.all_to_all(share.reshape(2, rows // 2, D), "core", 0, 0, tiled=True)
    share = jnp.sum(pair.astype(f32), axis=0).astype(bf16)
    shares = lax.all_to_all(share.reshape(NT // 2, rows // NT, D), "x", 0, 0, tiled=True)
    joined = jnp.sum(shares.astype(f32), axis=0).astype(bf16)
    twice = jnp.concatenate([joined, joined], axis=1)
    joined = lax.dynamic_slice_in_dim(twice, (NY - lax.axis_index("y")) % NY * (D // NY), D, axis=1)
    wide = joined.astype(f32)
    final_part = (wide * lax.rsqrt(row_squares(joined)[:, None] / D + eps) * final_gain).astype(bf16)
    final = lax.all_gather(final_part, TP, axis=0, tiled=True)

    logits = jnp.dot(final, head_all, preferred_element_type=f32)
    local_max = jnp.max(logits, axis=1)
    local_sum = jnp.sum(jnp.exp(logits - local_max[:, None]), axis=1)
    both = spread(jnp.stack([local_max, local_sum]), TP, NT)
    highest = jnp.max(both[:, 0], axis=0)
    total = jnp.sum(both[:, 1] * jnp.exp(both[:, 0] - highest), axis=0)
    return logits - highest[:, None] - jnp.log(total)[:, None]


def solution(mesh):
    mesh = Mesh(mesh.devices.reshape(NY, NZ, NT // 2, 2), FS + TP)
    return jax.shard_map(
        shards,
        mesh=mesh,
        in_specs=(
            P(FS, TP),
            P(FS),
            P(FS, TP),
            P(TP),
            P(TP),
            P(TP, FS),
            P(TP, FS),
            P(),
            P(FS, TP),
        ),
        out_specs=P(FS, TP),
        check_vma=False,
    )
```

time: 181 us -> 151 us (0.83)
  waiting for transfers between devices: 40.3 us -> 7.99 us
  blocking collectives: 62.9 us -> 74.5 us
  starting transfers between devices: 48 us -> 38.8 us
    ppermute x3, waiting for transfers between devices: 17.5 us -> 0.01 us  [the longest x2 0.01 us: shards(): down3, up3 = (lax.ppermute(far, 'y', DOWN), lax.ppermute(far, 'y', UP))]
    ppermute x2, waiting for transfers between devices: 9.79 us -> 0.01 us  [shards(): down2, up2 = (lax.ppermute(down, 'y', DOWN), lax.ppermute(up, 'y', UP))]
    all_to_all x1, starting transfers between devices: 10.9 us -> 3.49 us  [spread(): return lax.all_to_all(copies, axes, 0, 0, tiled=True)]
    ppermute x3, starting transfers between devices: 8.39 us -> 14.8 us  [the longest x1 8.27 us: shards(): far = lax.ppermute(own, 'y', ACROSS)]
    all_to_all x1, starting transfers between devices: 9.71 us -> 4.43 us  [shards(): lax.all_to_all(share.reshape(NT // 2, rows // NT, D), 'x', 0, 0, tiled=True)]
    all_to_all x1, waiting for transfers between devices: 12.3 us -> 7.25 us  [shards(): lax.all_to_all(share.reshape(NT // 2, rows // NT, D), 'x', 0, 0, tiled=True)]
    all_gather x1, blocking collectives: 23.3 us -> 28 us  [shards(): line = lax.all_gather(jnp.concatenate([own, far, low], axis=0), 'z', axis=0)]
    all_to_all x0 -> x1, blocking collectives: none -> 4.6 us  [shards(): lax.all_to_all(share.reshape(2, rows // 2, D), 'core', 0, 0, tiled=True)]
  transfers between devices with their start and end apart: 11 -> 11, of which waited for: 5 -> 1; matrix products, arithmetic and copies ran while one was open for 3% -> 5% of each run, Pallas kernels for 1% -> 1%
where the time goes in v2:
time: 151 us; the launch traced here: 150 us
  blocking collectives  74.5 us (49%)
  starting transfers between devices  38.8 us (26%)
  between operations  13.7 us (9%)
  waiting for transfers between devices  7.99 us (5%)
  matrix products  7.28 us (5%)
  other arithmetic  4.46 us (3%)
  local copies, waits for them, and re-layouts  2.45 us (2%)
    all_gather x1, blocking collectives, shards(): line = lax.all_gather(jnp.concatenate([own, far, low], axis=0), 'z', axis=0)  28 us
    psum x1, blocking collectives, shards(): squares = lax.psum(squares, TP)  19.6 us
    all_gather x1, blocking collectives, shards(): final = lax.all_gather(final_part, TP, axis=0, tiled=True)  15 us
    ppermute x1, starting transfers between devices, shards(): far = lax.ppermute(own, 'y', ACROSS)  8.27 us
    all_to_all x1, blocking collectives, spread(): return lax.all_to_all(copies, axes, 0, 0, tiled=True)  7.35 us
    all_to_all x1, waiting for transfers between devices, shards(): lax.all_to_all(share.reshape(NT // 2, rows // NT, D), 'x', 0, 0, tiled=True)  7.25 us
    ppermute x2, starting transfers between devices, shards(): down, up = (lax.ppermute(line, 'y', DOWN), lax.ppermute(line, 'y', UP))  7.17 us
    ppermute x2, starting transfers between devices, shards(): down3, up3 = (lax.ppermute(far, 'y', DOWN), lax.ppermute(far, 'y', UP))  6.5 us
  transfers between devices with their start and end apart: 11, of which 1 were waited for; matrix products, arithmetic and copies ran while one was open for 5% of the time, Pallas kernels for 1%

profile of v2, /device:TPU:1, one launch (start us, length us, event | category | flops | bytes accessed | tf_op | source)
XLA Modules:
  0.0 150.1 jit_solution(9400648390865554432)
XLA Ops:
  6.5 0.0 copy-start.2
  6.5 0.0 copy-start.1
  6.5 0.0 copy-start.6
  6.5 0.0 all-gather.3.cloned.1.call-start
  6.5 0.7 all-gather.3.cloned.1.call-update
  7.3 0.7 pad_maximum_fusion.1
  8.0 8.3 %collective-permute-start = (bf16[64,256]{1,0:T(8,128)(2,1)S(1)}, bf16[64,256]{1,0:T(8,128)(2,1)S(1)}, u32[]{:S(2)}, u32[]{:S(2)}) collective-permute-start(bf16[64,256]{1,0:T(8,128)(2,1)S(1)} %pad_maximum_fusion.1), channel_id=1, source_target_pairs={{0,256},{64,320},{128,384},{192,448},{256,0},{320,64},{384,128},{4... | collective-permute-start | bytes 98312 | tf_op jit(solution)/shard_map/ppermute | solution.py:73
  16.3 1.7 %broadcast_in_dim.4 = bf16[8,128,256]{2,1,0:T(8,128)(2,1)} broadcast(bf16[128,256]{1,0:T(8,128)(2,1)} %param.11), dimensions={1,2} | broadcast | bytes 589824 | tf_op jit(solution)/shard_map/broadcast_in_dim | solution.py:27
  17.9 3.5 %all-to-all-start = ((bf16[8,128,256]{2,1,0:T(8,128)(2,1)}), bf16[8,128,256]{2,1,0:T(8,128)(2,1)S(1)}, u32[]{:S(2)}, u32[]{:S(2)}) async-start(bf16[8,128,256]{2,1,0:T(8,128)(2,1)} %broadcast_in_dim.4), calls=%async_computation | async-start | bytes 1048576 | tf_op jit(solution)/shard_map/all_to_all | solution.py:28
  21.5 0.0 copy-done.6
  21.5 0.1 reshape.191
  21.6 0.1 reshape.192
  21.7 0.0 collective-permute-done
  21.7 0.0 copy-done.2
  21.7 0.0 copy-done.1
  21.8 28.0 %all-gather = bf16[1152,256]{1,0:T(8,128)(2,1)S(1)} all-gather(bf16[144,256]{1,0:T(8,128)(2,1)S(1)} %pad_maximum_fusion), channel_id=2, replica_groups=mesh['y'=8,'z'=8,'x'=4,'core'=2] {'z'}, dimensions={0}, use_global_device_ids=true | all-gather | bytes 663552 | tf_op jit(solution)/shard_map/all_gather | solution.py:74
  49.7 0.0 all-to-all-done
  49.8 0.1 add.90
  49.9 2.0 %fusion.4 = bf16[1536,256]{1,0:T(8,128)(2,1)} fusion(bf16[1024,256]{1,0:T(8,128)(2,1)S(1)} %bitcast.42, s32[1024]{0:T(1024)S(1)} %fusion.32, s32[1536]{0:T(1024)S(1)} %add.90), kind=kOutput, calls=%fused_computation.4 | convolution fusion | flops 807272448 | bytes 1320960 | tf_op jit(solution)/shard_map/dot_general | solution.py:84
  51.9 0.0 copy-start
  51.9 3.7 %all-to-all-start.1 = ((bf16[8,192,256]{2,1,0:T(8,128)(2,1)}), bf16[8,192,256]{2,1,0:T(8,128)(2,1)S(1)}, u32[]{:S(2)}, u32[]{:S(2)}) async-start(bf16[8,192,256]{2,1,0:T(8,128)(2,1)} %bitcast.5), calls=%async_computation.1 | async-start | bytes 1572864 | tf_op jit(solution)/shard_map/all_to_all | solution.py:85
  55.6 0.0 copy-start.4
  55.6 0.0 copy-start.5
  55.6 5.3 %collective-permute-start.1 = (bf16[8,64,256]{2,1,0:T(8,128)(2,1)S(1)}, bf16[8,64,256]{2,1,0:T(8,128)(2,1)S(1)}, u32[]{:S(2)}, u32[]{:S(2)}) collective-permute-start(bf16[8,64,256]{2,1,0:T(8,128)(2,1)S(1)} %get-tuple-element.12.refs_0_), channel_id=1, source_target_pairs={{0,448},{64,0},{128,64},{192,128},{256,192},{320,256},{384,320},{4... | collective-permute-start | bytes 786440 | tf_op jit(solution)/shard_map/ppermute | solution.py:80
  60.9 1.9 %collective-permute-start.5 = (bf16[8,64,256]{2,1,0:T(8,128)(2,1)S(1)}, bf16[8,64,256]{2,1,0:T(8,128)(2,1)S(1)}, u32[]{:S(2)}, u32[]{:S(2)}) collective-permute-start(bf16[8,64,256]{2,1,0:T(8,128)(2,1)S(1)} %get-tuple-element.12.refs_0_), channel_id=1, source_target_pairs={{0,64},{64,128},{128,192},{192,256},{256,320},{320,384},{384,448},... | collective-permute-start | bytes 786440 | tf_op jit(solution)/shard_map/ppermute | solution.py:80
  62.8 0.0 copy-done
  62.9 0.1 multiply_reduce_fusion
  63.0 0.1 reduce_sum.85
  63.1 0.1 stack.26
  63.2 1.9 %collective-permute-start.3 = (bf16[8,64,256]{2,1,0:T(8,128)(2,1)S(1)}, bf16[8,64,256]{2,1,0:T(8,128)(2,1)S(1)}, u32[]{:S(2)}, u32[]{:S(2)}) collective-permute-start(bf16[8,64,256]{2,1,0:T(8,128)(2,1)S(1)} %get-tuple-element.11.refs_4_), channel_id=1, source_target_pairs={{0,64},{64,128},{128,192},{192,256},{256,320},{320,384},{384,448},... | collective-permute-start | bytes 786440 | tf_op jit(solution)/shard_map/ppermute | solution.py:87
  65.1 4.6 %collective-permute-start.4 = (bf16[8,64,256]{2,1,0:T(8,128)(2,1)S(1)}, bf16[8,64,256]{2,1,0:T(8,128)(2,1)S(1)}, u32[]{:S(2)}, u32[]{:S(2)}) collective-permute-start(bf16[8,64,256]{2,1,0:T(8,128)(2,1)S(1)} %get-tuple-element.11.refs_4_), channel_id=1, source_target_pairs={{0,448},{64,0},{128,64},{192,128},{256,192},{320,256},{384,320},{4... | collective-permute-start | bytes 786440 | tf_op jit(solution)/shard_map/ppermute | solution.py:87
  69.7 0.0 collective-permute-done.1.refs_1_
  69.7 3.4 %collective-permute-start.2 = (bf16[8,64,256]{2,1,0:T(8,128)(2,1)S(1)}, bf16[8,64,256]{2,1,0:T(8,128)(2,1)S(1)}, u32[]{:S(2)}, u32[]{:S(2)}) collective-permute-start(bf16[8,64,256]{2,1,0:T(8,128)(2,1)S(1)} %collective-permute-done.1.refs_1_), channel_id=1, source_target_pairs={{0,448},{64,0},{128,64},{192,128},{256,192},{320,256},{384,320},{4... | collective-permute-start | bytes 786440 | tf_op jit(solution)/shard_map/ppermute | solution.py:86
  73.0 0.0 collective-permute-done.5.refs_7_
  73.1 1.9 %collective-permute-start.6 = (bf16[8,64,256]{2,1,0:T(8,128)(2,1)S(1)}, bf16[8,64,256]{2,1,0:T(8,128)(2,1)S(1)}, u32[]{:S(2)}, u32[]{:S(2)}) collective-permute-start(bf16[8,64,256]{2,1,0:T(8,128)(2,1)S(1)} %collective-permute-done.5.refs_7_), channel_id=1, source_target_pairs={{0,64},{64,128},{128,192},{192,256},{256,320},{320,384},{384,448},... | collective-permute-start | bytes 786440 | tf_op jit(solution)/shard_map/ppermute | solution.py:86
  75.0 0.0 all-to-all-done.1
  75.0 0.1 convert_reduce_fusion
  75.1 0.0 copy-done.4
  75.1 0.0 copy-done.5
  75.1 0.1 multiply_reduce_fusion.1
  75.3 19.6 %psum.7 = f32[2,192]{1,0:T(2,128)S(1)} all-reduce(f32[2,192]{1,0:T(2,128)S(1)} %pad_maximum_fusion.2), channel_id=1, replica_groups=mesh['y'=8,'z'=8,'x'=4,'core'=2] {'x','core'}, use_global_device_ids=true, to_apply=%region_3.4 | all-reduce | flops 384 | bytes 3072 | tf_op jit(solution)/shard_map/psum | solution.py:92
  94.9 0.1 copy.30.embed_scale_ref
  95.0 0.1 copy.31.hidden_scale_ref
  95.1 0.0 collective-permute-done.3.refs_3_
  95.1 0.0 collective-permute-done.4.refs_5_
  95.2 0.0 collective-permute-done.2.refs_2_
  95.2 0.0 collective-permute-done.6.refs_6_
  95.2 0.9 shard_map.91
  96.0 4.6 %all_to_all.25 = bf16[2,96,2048]{2,1,0:T(8,128)(2,1)S(1)} all-to-all(bf16[2,96,2048]{2,1,0:T(8,128)(2,1)S(1)} %bitcast.39), channel_id=1, replica_groups=mesh['y'=8,'z'=8,'x'=4,'core'=2] {'core'}, dimensions={0} | all-to-all | bytes 1572864 | tf_op jit(solution)/shard_map/all_to_all | solution.py:97
  100.6 0.0 copy-start.3
  100.6 1.0 reduce_sum.87
  101.6 4.4 %all-to-all-start.3 = ((bf16[4,24,2048]{2,1,0:T(8,128)(2,1)}), bf16[4,24,2048]{2,1,0:T(8,128)(2,1)S(1)}, u32[]{:S(2)}, u32[]{:S(2)}) async-start(bf16[4,24,2048]{2,1,0:T(8,128)(2,1)} %bitcast.14), calls=%async_computation.3 | async-start | bytes 786432 | tf_op jit(solution)/shard_map/all_to_all | solution.py:99
  106.0 7.3 %all-to-all-done.3 = bf16[4,24,2048]{2,1,0:T(8,128)(2,1)S(1)} async-done(((bf16[4,24,2048]{2,1,0:T(8,128)(2,1)}), bf16[4,24,2048]{2,1,0:T(8,128)(2,1)S(1)}, u32[]{:S(2)}, u32[]{:S(2)}) %all-to-all-start.3) | async-done | bytes 393248 | tf_op jit(solution)/shard_map/all_to_all | solution.py:99
  113.3 0.1 reduce_sum.88
  113.4 0.2 fusion.7
  113.6 0.0 copy-done.3
  113.6 0.1 fusion.9
  113.8 15.0 %all_gather.14 = bf16[192,2048]{1,0:T(8,128)(2,1)S(1)} all-gather(bf16[24,2048]{1,0:T(8,128)(2,1)S(1)} %fusion.9), channel_id=1, replica_groups=mesh['y'=8,'z'=8,'x'=4,'core'=2] {'x','core'}, dimensions={0}, use_global_device_ids=true | all-gather | bytes 884736 | tf_op jit(solution)/shard_map/all_gather | solution.py:105
  128.8 0.0 all-gather.3.cloned.1.call-done
  128.8 5.3 %fusion.37 = (f32[192]{0:T(256)S(1)}, f32[192,2048]{1,0:T(8,128)S(1)}) fusion(bf16[192,2048]{1,0:T(8,128)(2,1)S(1)} %all_gather.14, bf16[2048,2048]{1,0:T(8,128)(2,1)} %all-gather.3.cloned.1.call-done), kind=kOutput, calls=%fused_computation.70 | convolution fusion | flops 1611005696 | bytes 10748672 | tf_op jit(solution)/shard_map/dot_general | solution.py:107
  134.0 0.4 exponential_reduce_fusion
  134.4 7.4 %all_to_all.26 = f32[8,2,192]{2,1,0:T(2,128)S(1)} all-to-all(f32[8,2,192]{2,1,0:T(2,128)S(1)} %broadcast_in_dim.5), channel_id=1, replica_groups=mesh['y'=8,'z'=8,'x'=4,'core'=2] {'x','core'}, dimensions={0} | all-to-all | bytes 24576 | tf_op jit(solution)/shard_map/all_to_all | solution.py:28
  141.9 1.4 subtract_subtract_fusion
  (20 shorter events, 0.3 us)
Async XLA Ops:
  6.5 15.2 %copy-start.2 = (bf16[256,32]{0,1:T(8,128)(2,1)S(1)}, bf16[256,32]{0,1:T(8,128)(2,1)}, u32[]{:S(2)}) copy-start(bf16[256,32]{0,1:T(8,128)(2,1)} %param.14) | copy-start | bytes 49156
  6.5 15.2 %copy-start.1 = (bf16[256,32]{0,1:T(8,128)(2,1)S(1)}, bf16[256,32]{0,1:T(8,128)(2,1)}, u32[]{:S(2)}) copy-start(bf16[256,32]{0,1:T(8,128)(2,1)} %param.15) | copy-start | bytes 49156
  6.5 14.9 %copy-start.6 = (s32[192]{0:T(256)S(1)}, s32[192]{0:T(256)}, u32[]{:S(2)}) copy-start(s32[192]{0:T(256)} %param.10) | copy-start | bytes 2308
  6.5 122.2 %all-gather.3.cloned.1.call-start = ((), (), s32[]{:S(2)}) async-start(), calls=%async_computation.5 | async-start | bytes 8519680 | tf_op jit(solution)/shard_map/all_gather | solution.py:64
  8.0 13.7 %collective-permute-start = (bf16[64,256]{1,0:T(8,128)(2,1)S(1)}, bf16[64,256]{1,0:T(8,128)(2,1)S(1)}, u32[]{:S(2)}, u32[]{:S(2)}) collective-permute-start(bf16[64,256]{1,0:T(8,128)(2,1)S(1)} %pad_maximum_fusion.1), channel_id=1, source_target_pairs={{0,256},{64,320},{128,384},{192,448},{256,0},{320,64},{384,128},{4... | collective-permute-start | bytes 98312 | tf_op jit(solution)/shard_map/ppermute | solution.py:73
  17.9 31.8 %all-to-all-start = ((bf16[8,128,256]{2,1,0:T(8,128)(2,1)}), bf16[8,128,256]{2,1,0:T(8,128)(2,1)S(1)}, u32[]{:S(2)}, u32[]{:S(2)}) async-start(bf16[8,128,256]{2,1,0:T(8,128)(2,1)} %broadcast_in_dim.4), calls=%async_computation | async-start | bytes 1048576 | tf_op jit(solution)/shard_map/all_to_all | solution.py:28
  51.9 11.0 %copy-start = (bf16[192,256]{1,0:T(8,128)(2,1)S(1)}, bf16[192,256]{1,0:T(8,128)(2,1)}, u32[]{:S(2)}) copy-start(bf16[192,256]{1,0:T(8,128)(2,1)} %param.9) | copy-start | bytes 294916
  51.9 23.1 %all-to-all-start.1 = ((bf16[8,192,256]{2,1,0:T(8,128)(2,1)}), bf16[8,192,256]{2,1,0:T(8,128)(2,1)S(1)}, u32[]{:S(2)}, u32[]{:S(2)}) async-start(bf16[8,192,256]{2,1,0:T(8,128)(2,1)} %bitcast.5), calls=%async_computation.1 | async-start | bytes 1572864 | tf_op jit(solution)/shard_map/all_to_all | solution.py:85
  55.6 19.5 %copy-start.4 = (f32[256]{0:T(256)S(1)}, f32[256]{0:T(256)}, u32[]{:S(2)}) copy-start(f32[256]{0:T(256)} %param.12) | copy-start | bytes 3076
  55.6 19.5 %copy-start.5 = (f32[256]{0:T(256)S(1)}, f32[256]{0:T(256)}, u32[]{:S(2)}) copy-start(f32[256]{0:T(256)} %param.13) | copy-start | bytes 3076
  55.6 14.0 %collective-permute-start.1 = (bf16[8,64,256]{2,1,0:T(8,128)(2,1)S(1)}, bf16[8,64,256]{2,1,0:T(8,128)(2,1)S(1)}, u32[]{:S(2)}, u32[]{:S(2)}) collective-permute-start(bf16[8,64,256]{2,1,0:T(8,128)(2,1)S(1)} %get-tuple-element.12.refs_0_), channel_id=1, source_target_pairs={{0,448},{64,0},{128,64},{192,128},{256,192},{320,256},{384,320},{4... | collective-permute-start | bytes 786440 | tf_op jit(solution)/shard_map/ppermute | solution.py:80
  60.9 12.2 %collective-permute-start.5 = (bf16[8,64,256]{2,1,0:T(8,128)(2,1)S(1)}, bf16[8,64,256]{2,1,0:T(8,128)(2,1)S(1)}, u32[]{:S(2)}, u32[]{:S(2)}) collective-permute-start(bf16[8,64,256]{2,1,0:T(8,128)(2,1)S(1)} %get-tuple-element.12.refs_0_), channel_id=1, source_target_pairs={{0,64},{64,128},{128,192},{192,256},{256,320},{320,384},{384,448},... | collective-permute-start | bytes 786440 | tf_op jit(solution)/shard_map/ppermute | solution.py:80
  63.2 32.0 %collective-permute-start.3 = (bf16[8,64,256]{2,1,0:T(8,128)(2,1)S(1)}, bf16[8,64,256]{2,1,0:T(8,128)(2,1)S(1)}, u32[]{:S(2)}, u32[]{:S(2)}) collective-permute-start(bf16[8,64,256]{2,1,0:T(8,128)(2,1)S(1)} %get-tuple-element.11.refs_4_), channel_id=1, source_target_pairs={{0,64},{64,128},{128,192},{192,256},{256,320},{320,384},{384,448},... | collective-permute-start | bytes 786440 | tf_op jit(solution)/shard_map/ppermute | solution.py:87
  65.1 30.1 %collective-permute-start.4 = (bf16[8,64,256]{2,1,0:T(8,128)(2,1)S(1)}, bf16[8,64,256]{2,1,0:T(8,128)(2,1)S(1)}, u32[]{:S(2)}, u32[]{:S(2)}) collective-permute-start(bf16[8,64,256]{2,1,0:T(8,128)(2,1)S(1)} %get-tuple-element.11.refs_4_), channel_id=1, source_target_pairs={{0,448},{64,0},{128,64},{192,128},{256,192},{320,256},{384,320},{4... | collective-permute-start | bytes 786440 | tf_op jit(solution)/shard_map/ppermute | solution.py:87
  69.7 25.5 %collective-permute-start.2 = (bf16[8,64,256]{2,1,0:T(8,128)(2,1)S(1)}, bf16[8,64,256]{2,1,0:T(8,128)(2,1)S(1)}, u32[]{:S(2)}, u32[]{:S(2)}) collective-permute-start(bf16[8,64,256]{2,1,0:T(8,128)(2,1)S(1)} %collective-permute-done.1.refs_1_), channel_id=1, source_target_pairs={{0,448},{64,0},{128,64},{192,128},{256,192},{320,256},{384,320},{4... | collective-permute-start | bytes 786440 | tf_op jit(solution)/shard_map/ppermute | solution.py:86
  73.1 22.1 %collective-permute-start.6 = (bf16[8,64,256]{2,1,0:T(8,128)(2,1)S(1)}, bf16[8,64,256]{2,1,0:T(8,128)(2,1)S(1)}, u32[]{:S(2)}, u32[]{:S(2)}) collective-permute-start(bf16[8,64,256]{2,1,0:T(8,128)(2,1)S(1)} %collective-permute-done.5.refs_7_), channel_id=1, source_target_pairs={{0,64},{64,128},{128,192},{192,256},{256,320},{320,384},{384,448},... | collective-permute-start | bytes 786440 | tf_op jit(solution)/shard_map/ppermute | solution.py:86
  100.6 13.0 %copy-start.3 = (f32[2048]{0:T(1024)S(1)}, f32[2048]{0:T(1024)}, u32[]{:S(2)}) copy-start(f32[2048]{0:T(1024)} %param.16) | copy-start | bytes 24580
  101.6 11.7 %all-to-all-start.3 = ((bf16[4,24,2048]{2,1,0:T(8,128)(2,1)}), bf16[4,24,2048]{2,1,0:T(8,128)(2,1)S(1)}, u32[]{:S(2)}, u32[]{:S(2)}) async-start(bf16[4,24,2048]{2,1,0:T(8,128)(2,1)} %bitcast.14), calls=%async_computation.3 | async-start | bytes 786432 | tf_op jit(solution)/shard_map/all_to_all | solution.py:99
Sparse Core Ops, SparseCore 0:
  10.4 113.8 all-gather.2

commit v3 on v2

--- a/solution.py
+++ b/solution.py
@@ -89,7 +89,7 @@
 
     embedded = jnp.sum(found.astype(f32), axis=0)
     squares = jnp.stack([row_squares(embedded), row_squares(hidden_prev)])
-    squares = lax.psum(squares, TP)
+    squares = lax.psum(lax.optimization_barrier(lax.psum(squares, "core")), "x")
     scales = lax.rsqrt(squares / D + eps)[:, :, None]
     embedded = (embedded * embed_gain).astype(bf16)
     hidden = (hidden_prev.astype(f32) * hidden_gain).astype(bf16)

time: 151 us -> 151 us (level)
    psum x1 -> x2, blocking collectives: 19.6 us -> 18.9 us  [shards(): squares = lax.psum(lax.optimization_barrier(lax.psum(squares, 'core')), 'x')]
where the time goes in v3:
time: 151 us; the launch traced here: 150 us
  blocking collectives  74.7 us (49%)
  starting transfers between devices  38.6 us (26%)
  between operations  13.7 us (9%)
  waiting for transfers between devices  7.99 us (5%)
  matrix products  7.28 us (5%)
  other arithmetic  4.46 us (3%)
  local copies, waits for them, and re-layouts  2.44 us (2%)
    all_gather x1, blocking collectives, shards(): line = lax.all_gather(jnp.concatenate([own, far, low], axis=0), 'z', axis=0)  28 us
    psum x2, blocking collectives, shards(): squares = lax.psum(lax.optimization_barrier(lax.psum(squares, 'core')), 'x')  18.9 us
    all_gather x1, blocking collectives, shards(): final = lax.all_gather(final_part, TP, axis=0, tiled=True)  15 us
    ppermute x1, starting transfers between devices, shards(): far = lax.ppermute(own, 'y', ACROSS)  8.27 us
    all_to_all x1, blocking collectives, spread(): return lax.all_to_all(copies, axes, 0, 0, tiled=True)  7.35 us
    all_to_all x1, waiting for transfers between devices, shards(): lax.all_to_all(share.reshape(NT // 2, rows // NT, D), 'x', 0, 0, tiled=True)  7.25 us
    ppermute x2, starting transfers between devices, shards(): down, up = (lax.ppermute(line, 'y', DOWN), lax.ppermute(line, 'y', UP))  7.17 us
    ppermute x2, starting transfers between devices, shards(): down3, up3 = (lax.ppermute(far, 'y', DOWN), lax.ppermute(far, 'y', UP))  6.5 us
  transfers between devices with their start and end apart: 11, of which 1 were waited for; matrix products, arithmetic and copies ran while one was open for 5% of the time, Pallas kernels for 1%

profile of v3, /device:TPU:1, one launch (start us, length us, event | category | flops | bytes accessed | tf_op | source)
XLA Modules:
  0.0 150.1 jit_solution(2851628761219366390)
XLA Ops:
  6.5 0.0 copy-start.2
  6.5 0.0 copy-start.1
  6.5 0.0 copy-start.6
  6.5 0.0 all-gather.3.cloned.1.call-start
  6.5 0.7 all-gather.3.cloned.1.call-update
  7.3 0.7 pad_maximum_fusion.1
  8.0 8.3 %collective-permute-start = (bf16[64,256]{1,0:T(8,128)(2,1)S(1)}, bf16[64,256]{1,0:T(8,128)(2,1)S(1)}, u32[]{:S(2)}, u32[]{:S(2)}) collective-permute-start(bf16[64,256]{1,0:T(8,128)(2,1)S(1)} %pad_maximum_fusion.1), channel_id=1, source_target_pairs={{0,256},{64,320},{128,384},{192,448},{256,0},{320,64},{384,128},{4... | collective-permute-start | bytes 98312 | tf_op jit(solution)/shard_map/ppermute | solution.py:73
  16.3 1.7 %broadcast_in_dim.4 = bf16[8,128,256]{2,1,0:T(8,128)(2,1)} broadcast(bf16[128,256]{1,0:T(8,128)(2,1)} %param.11), dimensions={1,2} | broadcast | bytes 589824 | tf_op jit(solution)/shard_map/broadcast_in_dim | solution.py:27
  17.9 3.5 %all-to-all-start = ((bf16[8,128,256]{2,1,0:T(8,128)(2,1)}), bf16[8,128,256]{2,1,0:T(8,128)(2,1)S(1)}, u32[]{:S(2)}, u32[]{:S(2)}) async-start(bf16[8,128,256]{2,1,0:T(8,128)(2,1)} %broadcast_in_dim.4), calls=%async_computation | async-start | bytes 1048576 | tf_op jit(solution)/shard_map/all_to_all | solution.py:28
  21.5 0.0 copy-done.6
  21.5 0.1 reshape.191
  21.6 0.1 reshape.192
  21.7 0.0 collective-permute-done
  21.7 0.0 copy-done.2
  21.7 0.0 copy-done.1
  21.8 28.0 %all-gather = bf16[1152,256]{1,0:T(8,128)(2,1)S(1)} all-gather(bf16[144,256]{1,0:T(8,128)(2,1)S(1)} %pad_maximum_fusion), channel_id=2, replica_groups=mesh['y'=8,'z'=8,'x'=4,'core'=2] {'z'}, dimensions={0}, use_global_device_ids=true | all-gather | bytes 663552 | tf_op jit(solution)/shard_map/all_gather | solution.py:74
  49.7 0.0 all-to-all-done
  49.8 0.1 add.92
  49.9 2.0 %fusion.4 = bf16[1536,256]{1,0:T(8,128)(2,1)} fusion(bf16[1024,256]{1,0:T(8,128)(2,1)S(1)} %bitcast.42, s32[1024]{0:T(1024)S(1)} %fusion.32, s32[1536]{0:T(1024)S(1)} %add.92), kind=kOutput, calls=%fused_computation.4 | convolution fusion | flops 807272448 | bytes 1320960 | tf_op jit(solution)/shard_map/dot_general | solution.py:84
  51.9 0.0 copy-start
  51.9 3.7 %all-to-all-start.1 = ((bf16[8,192,256]{2,1,0:T(8,128)(2,1)}), bf16[8,192,256]{2,1,0:T(8,128)(2,1)S(1)}, u32[]{:S(2)}, u32[]{:S(2)}) async-start(bf16[8,192,256]{2,1,0:T(8,128)(2,1)} %bitcast.5), calls=%async_computation.1 | async-start | bytes 1572864 | tf_op jit(solution)/shard_map/all_to_all | solution.py:85
  55.6 0.0 copy-start.4
  55.6 0.0 copy-start.5
  55.6 5.3 %collective-permute-start.1 = (bf16[8,64,256]{2,1,0:T(8,128)(2,1)S(1)}, bf16[8,64,256]{2,1,0:T(8,128)(2,1)S(1)}, u32[]{:S(2)}, u32[]{:S(2)}) collective-permute-start(bf16[8,64,256]{2,1,0:T(8,128)(2,1)S(1)} %get-tuple-element.12.refs_0_), channel_id=1, source_target_pairs={{0,448},{64,0},{128,64},{192,128},{256,192},{320,256},{384,320},{4... | collective-permute-start | bytes 786440 | tf_op jit(solution)/shard_map/ppermute | solution.py:80
  60.9 1.9 %collective-permute-start.5 = (bf16[8,64,256]{2,1,0:T(8,128)(2,1)S(1)}, bf16[8,64,256]{2,1,0:T(8,128)(2,1)S(1)}, u32[]{:S(2)}, u32[]{:S(2)}) collective-permute-start(bf16[8,64,256]{2,1,0:T(8,128)(2,1)S(1)} %get-tuple-element.12.refs_0_), channel_id=1, source_target_pairs={{0,64},{64,128},{128,192},{192,256},{256,320},{320,384},{384,448},... | collective-permute-start | bytes 786440 | tf_op jit(solution)/shard_map/ppermute | solution.py:80
  62.8 0.0 copy-done
  62.9 0.1 multiply_reduce_fusion
  63.0 0.1 reduce_sum.85
  63.1 0.1 stack.26
  63.1 1.9 %collective-permute-start.3 = (bf16[8,64,256]{2,1,0:T(8,128)(2,1)S(1)}, bf16[8,64,256]{2,1,0:T(8,128)(2,1)S(1)}, u32[]{:S(2)}, u32[]{:S(2)}) collective-permute-start(bf16[8,64,256]{2,1,0:T(8,128)(2,1)S(1)} %get-tuple-element.11.refs_4_), channel_id=1, source_target_pairs={{0,64},{64,128},{128,192},{192,256},{256,320},{320,384},{384,448},... | collective-permute-start | bytes 786440 | tf_op jit(solution)/shard_map/ppermute | solution.py:87
  65.1 4.6 %collective-permute-start.4 = (bf16[8,64,256]{2,1,0:T(8,128)(2,1)S(1)}, bf16[8,64,256]{2,1,0:T(8,128)(2,1)S(1)}, u32[]{:S(2)}, u32[]{:S(2)}) collective-permute-start(bf16[8,64,256]{2,1,0:T(8,128)(2,1)S(1)} %get-tuple-element.11.refs_4_), channel_id=1, source_target_pairs={{0,448},{64,0},{128,64},{192,128},{256,192},{320,256},{384,320},{4... | collective-permute-start | bytes 786440 | tf_op jit(solution)/shard_map/ppermute | solution.py:87
  69.7 0.0 collective-permute-done.1.refs_1_
  69.7 3.4 %collective-permute-start.2 = (bf16[8,64,256]{2,1,0:T(8,128)(2,1)S(1)}, bf16[8,64,256]{2,1,0:T(8,128)(2,1)S(1)}, u32[]{:S(2)}, u32[]{:S(2)}) collective-permute-start(bf16[8,64,256]{2,1,0:T(8,128)(2,1)S(1)} %collective-permute-done.1.refs_1_), channel_id=1, source_target_pairs={{0,448},{64,0},{128,64},{192,128},{256,192},{320,256},{384,320},{4... | collective-permute-start | bytes 786440 | tf_op jit(solution)/shard_map/ppermute | solution.py:86
  73.0 0.0 collective-permute-done.5.refs_7_
  73.1 1.9 %collective-permute-start.6 = (bf16[8,64,256]{2,1,0:T(8,128)(2,1)S(1)}, bf16[8,64,256]{2,1,0:T(8,128)(2,1)S(1)}, u32[]{:S(2)}, u32[]{:S(2)}) collective-permute-start(bf16[8,64,256]{2,1,0:T(8,128)(2,1)S(1)} %collective-permute-done.5.refs_7_), channel_id=1, source_target_pairs={{0,64},{64,128},{128,192},{192,256},{256,320},{320,384},{384,448},... | collective-permute-start | bytes 786440 | tf_op jit(solution)/shard_map/ppermute | solution.py:86
  75.0 0.0 all-to-all-done.1
  75.0 0.1 convert_reduce_fusion
  75.1 0.0 copy-done.4
  75.1 0.0 copy-done.5
  75.1 0.1 multiply_reduce_fusion.1
  75.3 9.1 %psum.14 = f32[2,192]{1,0:T(2,128)S(1)} all-reduce(f32[2,192]{1,0:T(2,128)S(1)} %pad_maximum_fusion.2), channel_id=1, replica_groups=mesh['y'=8,'z'=8,'x'=4,'core'=2] {'core'}, use_global_device_ids=true, to_apply=%region_3.4 | all-reduce | flops 384 | bytes 3072 | tf_op jit(solution)/shard_map/psum | solution.py:92
  84.4 9.8 %psum.15 = f32[2,192]{1,0:T(2,128)S(1)} all-reduce(f32[2,192]{1,0:T(2,128)S(1)} %psum.14), channel_id=1, replica_groups=mesh['y'=8,'z'=8,'x'=4,'core'=2] {'x'}, use_global_device_ids=true, to_apply=%region_4.5 | all-reduce | flops 384 | bytes 3072 | tf_op jit(solution)/shard_map/psum | solution.py:92
  94.1 0.1 copy.30.embed_scale_ref
  94.3 0.1 copy.31.hidden_scale_ref
  94.4 0.0 collective-permute-done.3.refs_3_
  94.4 0.0 collective-permute-done.4.refs_5_
  94.4 0.0 collective-permute-done.2.refs_2_
  94.4 0.0 collective-permute-done.6.refs_6_
  94.4 0.8 shard_map.91
  95.3 5.6 %all_to_all.25 = bf16[2,96,2048]{2,1,0:T(8,128)(2,1)S(1)} all-to-all(bf16[2,96,2048]{2,1,0:T(8,128)(2,1)S(1)} %bitcast.39), channel_id=1, replica_groups=mesh['y'=8,'z'=8,'x'=4,'core'=2] {'core'}, dimensions={0} | all-to-all | bytes 1572864 | tf_op jit(solution)/shard_map/all_to_all | solution.py:97
  100.9 0.0 copy-start.3
  100.9 1.0 reduce_sum.87
  101.8 4.2 %all-to-all-start.3 = ((bf16[4,24,2048]{2,1,0:T(8,128)(2,1)}), bf16[4,24,2048]{2,1,0:T(8,128)(2,1)S(1)}, u32[]{:S(2)}, u32[]{:S(2)}) async-start(bf16[4,24,2048]{2,1,0:T(8,128)(2,1)} %bitcast.14), calls=%async_computation.3 | async-start | bytes 786432 | tf_op jit(solution)/shard_map/all_to_all | solution.py:99
  106.0 7.3 %all-to-all-done.3 = bf16[4,24,2048]{2,1,0:T(8,128)(2,1)S(1)} async-done(((bf16[4,24,2048]{2,1,0:T(8,128)(2,1)}), bf16[4,24,2048]{2,1,0:T(8,128)(2,1)S(1)}, u32[]{:S(2)}, u32[]{:S(2)}) %all-to-all-start.3) | async-done | bytes 393248 | tf_op jit(solution)/shard_map/all_to_all | solution.py:99
  113.3 0.1 reduce_sum.88
  113.4 0.2 fusion.7
  113.6 0.0 copy-done.3
  113.6 0.1 fusion.9
  113.8 15.0 %all_gather.14 = bf16[192,2048]{1,0:T(8,128)(2,1)S(1)} all-gather(bf16[24,2048]{1,0:T(8,128)(2,1)S(1)} %fusion.9), channel_id=1, replica_groups=mesh['y'=8,'z'=8,'x'=4,'core'=2] {'x','core'}, dimensions={0}, use_global_device_ids=true | all-gather | bytes 884736 | tf_op jit(solution)/shard_map/all_gather | solution.py:105
  128.8 0.0 all-gather.3.cloned.1.call-done
  128.8 5.3 %fusion.37 = (f32[192]{0:T(256)S(1)}, f32[192,2048]{1,0:T(8,128)S(1)}) fusion(bf16[192,2048]{1,0:T(8,128)(2,1)S(1)} %all_gather.14, bf16[2048,2048]{1,0:T(8,128)(2,1)} %all-gather.3.cloned.1.call-done), kind=kOutput, calls=%fused_computation.70 | convolution fusion | flops 1611005696 | bytes 10748672 | tf_op jit(solution)/shard_map/dot_general | solution.py:107
  134.0 0.4 exponential_reduce_fusion
  134.4 7.3 %all_to_all.26 = f32[8,2,192]{2,1,0:T(2,128)S(1)} all-to-all(f32[8,2,192]{2,1,0:T(2,128)S(1)} %broadcast_in_dim.5), channel_id=1, replica_groups=mesh['y'=8,'z'=8,'x'=4,'core'=2] {'x','core'}, dimensions={0} | all-to-all | bytes 24576 | tf_op jit(solution)/shard_map/all_to_all | solution.py:28
  141.8 1.4 subtract_subtract_fusion
  (20 shorter events, 0.3 us)
Async XLA Ops:
  6.5 15.2 %copy-start.2 = (bf16[256,32]{0,1:T(8,128)(2,1)S(1)}, bf16[256,32]{0,1:T(8,128)(2,1)}, u32[]{:S(2)}) copy-start(bf16[256,32]{0,1:T(8,128)(2,1)} %param.14) | copy-start | bytes 49156
  6.5 15.2 %copy-start.1 = (bf16[256,32]{0,1:T(8,128)(2,1)S(1)}, bf16[256,32]{0,1:T(8,128)(2,1)}, u32[]{:S(2)}) copy-start(bf16[256,32]{0,1:T(8,128)(2,1)} %param.15) | copy-start | bytes 49156
  6.5 14.9 %copy-start.6 = (s32[192]{0:T(256)S(1)}, s32[192]{0:T(256)}, u32[]{:S(2)}) copy-start(s32[192]{0:T(256)} %param.10) | copy-start | bytes 2308
  6.5 122.2 %all-gather.3.cloned.1.call-start = ((), (), s32[]{:S(2)}) async-start(), calls=%async_computation.5 | async-start | bytes 8519680 | tf_op jit(solution)/shard_map/all_gather | solution.py:64
  8.0 13.7 %collective-permute-start = (bf16[64,256]{1,0:T(8,128)(2,1)S(1)}, bf16[64,256]{1,0:T(8,128)(2,1)S(1)}, u32[]{:S(2)}, u32[]{:S(2)}) collective-permute-start(bf16[64,256]{1,0:T(8,128)(2,1)S(1)} %pad_maximum_fusion.1), channel_id=1, source_target_pairs={{0,256},{64,320},{128,384},{192,448},{256,0},{320,64},{384,128},{4... | collective-permute-start | bytes 98312 | tf_op jit(solution)/shard_map/ppermute | solution.py:73
  17.9 31.8 %all-to-all-start = ((bf16[8,128,256]{2,1,0:T(8,128)(2,1)}), bf16[8,128,256]{2,1,0:T(8,128)(2,1)S(1)}, u32[]{:S(2)}, u32[]{:S(2)}) async-start(bf16[8,128,256]{2,1,0:T(8,128)(2,1)} %broadcast_in_dim.4), calls=%async_computation | async-start | bytes 1048576 | tf_op jit(solution)/shard_map/all_to_all | solution.py:28
  51.9 11.0 %copy-start = (bf16[192,256]{1,0:T(8,128)(2,1)S(1)}, bf16[192,256]{1,0:T(8,128)(2,1)}, u32[]{:S(2)}) copy-start(bf16[192,256]{1,0:T(8,128)(2,1)} %param.9) | copy-start | bytes 294916
  51.9 23.1 %all-to-all-start.1 = ((bf16[8,192,256]{2,1,0:T(8,128)(2,1)}), bf16[8,192,256]{2,1,0:T(8,128)(2,1)S(1)}, u32[]{:S(2)}, u32[]{:S(2)}) async-start(bf16[8,192,256]{2,1,0:T(8,128)(2,1)} %bitcast.5), calls=%async_computation.1 | async-start | bytes 1572864 | tf_op jit(solution)/shard_map/all_to_all | solution.py:85
  55.6 19.5 %copy-start.4 = (f32[256]{0:T(256)S(1)}, f32[256]{0:T(256)}, u32[]{:S(2)}) copy-start(f32[256]{0:T(256)} %param.12) | copy-start | bytes 3076
  55.6 19.5 %copy-start.5 = (f32[256]{0:T(256)S(1)}, f32[256]{0:T(256)}, u32[]{:S(2)}) copy-start(f32[256]{0:T(256)} %param.13) | copy-start | bytes 3076
  55.6 14.0 %collective-permute-start.1 = (bf16[8,64,256]{2,1,0:T(8,128)(2,1)S(1)}, bf16[8,64,256]{2,1,0:T(8,128)(2,1)S(1)}, u32[]{:S(2)}, u32[]{:S(2)}) collective-permute-start(bf16[8,64,256]{2,1,0:T(8,128)(2,1)S(1)} %get-tuple-element.12.refs_0_), channel_id=1, source_target_pairs={{0,448},{64,0},{128,64},{192,128},{256,192},{320,256},{384,320},{4... | collective-permute-start | bytes 786440 | tf_op jit(solution)/shard_map/ppermute | solution.py:80
  60.9 12.2 %collective-permute-start.5 = (bf16[8,64,256]{2,1,0:T(8,128)(2,1)S(1)}, bf16[8,64,256]{2,1,0:T(8,128)(2,1)S(1)}, u32[]{:S(2)}, u32[]{:S(2)}) collective-permute-start(bf16[8,64,256]{2,1,0:T(8,128)(2,1)S(1)} %get-tuple-element.12.refs_0_), channel_id=1, source_target_pairs={{0,64},{64,128},{128,192},{192,256},{256,320},{320,384},{384,448},... | collective-permute-start | bytes 786440 | tf_op jit(solution)/shard_map/ppermute | solution.py:80
  63.1 31.3 %collective-permute-start.3 = (bf16[8,64,256]{2,1,0:T(8,128)(2,1)S(1)}, bf16[8,64,256]{2,1,0:T(8,128)(2,1)S(1)}, u32[]{:S(2)}, u32[]{:S(2)}) collective-permute-start(bf16[8,64,256]{2,1,0:T(8,128)(2,1)S(1)} %get-tuple-element.11.refs_4_), channel_id=1, source_target_pairs={{0,64},{64,128},{128,192},{192,256},{256,320},{320,384},{384,448},... | collective-permute-start | bytes 786440 | tf_op jit(solution)/shard_map/ppermute | solution.py:87
  65.1 29.3 %collective-permute-start.4 = (bf16[8,64,256]{2,1,0:T(8,128)(2,1)S(1)}, bf16[8,64,256]{2,1,0:T(8,128)(2,1)S(1)}, u32[]{:S(2)}, u32[]{:S(2)}) collective-permute-start(bf16[8,64,256]{2,1,0:T(8,128)(2,1)S(1)} %get-tuple-element.11.refs_4_), channel_id=1, source_target_pairs={{0,448},{64,0},{128,64},{192,128},{256,192},{320,256},{384,320},{4... | collective-permute-start | bytes 786440 | tf_op jit(solution)/shard_map/ppermute | solution.py:87
  69.7 24.7 %collective-permute-start.2 = (bf16[8,64,256]{2,1,0:T(8,128)(2,1)S(1)}, bf16[8,64,256]{2,1,0:T(8,128)(2,1)S(1)}, u32[]{:S(2)}, u32[]{:S(2)}) collective-permute-start(bf16[8,64,256]{2,1,0:T(8,128)(2,1)S(1)} %collective-permute-done.1.refs_1_), channel_id=1, source_target_pairs={{0,448},{64,0},{128,64},{192,128},{256,192},{320,256},{384,320},{4... | collective-permute-start | bytes 786440 | tf_op jit(solution)/shard_map/ppermute | solution.py:86
  73.1 21.4 %collective-permute-start.6 = (bf16[8,64,256]{2,1,0:T(8,128)(2,1)S(1)}, bf16[8,64,256]{2,1,0:T(8,128)(2,1)S(1)}, u32[]{:S(2)}, u32[]{:S(2)}) collective-permute-start(bf16[8,64,256]{2,1,0:T(8,128)(2,1)S(1)} %collective-permute-done.5.refs_7_), channel_id=1, source_target_pairs={{0,64},{64,128},{128,192},{192,256},{256,320},{320,384},{384,448},... | collective-permute-start | bytes 786440 | tf_op jit(solution)/shard_map/ppermute | solution.py:86
  100.9 12.8 %copy-start.3 = (f32[2048]{0:T(1024)S(1)}, f32[2048]{0:T(1024)}, u32[]{:S(2)}) copy-start(f32[2048]{0:T(1024)} %param.16) | copy-start | bytes 24580
  101.8 11.4 %all-to-all-start.3 = ((bf16[4,24,2048]{2,1,0:T(8,128)(2,1)}), bf16[4,24,2048]{2,1,0:T(8,128)(2,1)S(1)}, u32[]{:S(2)}, u32[]{:S(2)}) async-start(bf16[4,24,2048]{2,1,0:T(8,128)(2,1)} %bitcast.14), calls=%async_computation.3 | async-start | bytes 786432 | tf_op jit(solution)/shard_map/all_to_all | solution.py:99
Sparse Core Ops, SparseCore 0:
  10.4 113.8 all-gather.2
